TPU v7x, 32 devices: a whole 2x2x4 slice. The times are simulated.
32 devices in a mesh: row: 4 (over y, x), col: 8 (over z, core).
Axes of the slice: x: 2, y: 2, z: 4, core: 2. Of those that a mesh axis runs over, the one named last changes fastest.
Arguments:
- sigma_anc: bfloat16 [8, 640, 5120], P(None, 'col', 'row'), may hold values from -6 to 6
- owner: int32 [8], replicated, may hold values from 0 to 7, as said below
- structure: int32 [8, 4], replicated, may hold values from 0 to 7, as said below
- factor: bfloat16 [8, 2560, 640], P('col', 'row'), may hold values from -0.125 to 0.125
- diag_inv: float32 [8, 640, 640], P('col', None, 'row'), may hold values from -6 to 6
Outputs:
- offdiag: bfloat16 [8, 2560, 640], P('col', 'row')
- diagblock: float32 [8, 640, 640], P('col', None, 'row')
Inputs may be any that keep to these rules, and one draw needn't show every extreme that they name: owner maps each group of 2 ancestors, j // 2 equal, one to one onto the stored columns of the same group. `structure`: entry a of every supernode's list lies between a * 2 and (a + 1) * 2 - 1.
All inputs are finite; a program needn't handle non-finite values.
Results may differ from a plain program's by a relative error of at most 0.014.
Values may be sent and summed in bfloat16 or wider, within the bound.
A program may use at most 64 MiB of HBM per device.

v0:
```python
import jax
import jax.numpy as jnp
from jax import lax
from jax.sharding import PartitionSpec as P


def body(sigma_anc, owner, structure, factor, diag_inv):
    here_row = lax.axis_index("row")
    block_width = factor.shape[2]
    groups = sigma_anc.shape[2] // block_width
    piece_rows = sigma_anc.shape[1]
    count_anc = sigma_anc.shape[0]
    flattened = sigma_anc.reshape(count_anc, piece_rows, groups, block_width).transpose(0, 2, 1, 3)
    flattened = flattened.reshape(count_anc * groups, piece_rows, block_width)
    target = lax.dynamic_index_in_dim(structure, here_row, axis=1, keepdims=False)
    column_here = jnp.take(owner, target) - here_row * groups
    indices = structure * groups + column_here[:, None]
    outgoing = jnp.take(flattened, indices.reshape(-1), axis=0)
    outgoing = outgoing.reshape(structure.shape[0], structure.shape[1], piece_rows, block_width)
    factor_block = factor[0]
    received = lax.all_to_all(outgoing, "col", split_axis=0, concat_axis=2, tiled=True)
    slot_terms = lax.dot_general(
        received[0], factor_block, (((2,), (0,)), ((), ())), preferred_element_type=jnp.float32
    )
    summed = lax.psum_scatter(
        slot_terms.reshape(-1, block_width).astype(jnp.bfloat16),
        "row",
        scatter_dimension=0,
        tiled=True,
    ).astype(jnp.float32)
    offdiag = (-summed).astype(jnp.bfloat16)
    partial_terms = lax.dot_general(
        factor_block, offdiag, (((0,), (0,)), ((), ())), preferred_element_type=jnp.float32
    )
    diagblock = diag_inv[0] - lax.psum_scatter(
        partial_terms.astype(jnp.bfloat16), "row", scatter_dimension=1, tiled=True
    ).astype(jnp.float32)
    return (offdiag[None], diagblock[None])


def solution(mesh):
    return jax.shard_map(
        body,
        mesh=mesh,
        in_specs=(P(None, "col", "row"), P(), P(), P("col", "row", None), P("col", None, "row")),
        out_specs=(P("col", "row", None), P("col", None, "row")),
        check_vma=False,
    )
```

profile of v0, /device:TPU:0, one launch (start us, length us, event | category | flops | bytes accessed | tf_op | source)
XLA Modules:
  0.0 185.1 jit_solution(5577912758673404686)
XLA Ops:
  7.2 0.0 copy-start
  7.2 0.0 reduce-scatter.3.cloned.1.call-start
  7.2 0.8 fusion.6
  8.0 1.3 gather_fusion
  9.3 0.7 subtract_bitcast_fusion
  10.0 0.7 compare_and_fusion
  10.7 0.1 copy.10
  10.8 0.1 copy.11
  10.9 0.1 reshape.58
  11.0 1.5 fusion.7
  12.5 0.1 pad_maximum_fusion
  12.6 2.6 %gather_fusion.1 = bf16[32,80,640]{2,1,0:T(8,128)(2,1)} fusion(bf16[16,80,640]{2,1,0:T(8,128)(2,1)S(1)} %bitcast.32, s32[1024]{0:T(1024)S(1)} %pad_clamp_fusion), kind=kCustom, calls=%fused_computation.1 | custom fusion | bytes 6553728 | tf_op jit(solution)/shard_map/jit(_take)/gather | solution.py:18
  15.3 2.3 %broadcast_select_fusion = bf16[8,4,80,640]{3,2,1,0:T(8,128)(2,1)S(1)} fusion(bf16[8,4,80,640]{3,2,1,0:T(8,128)(2,1)} %bitcast.34, pred[8,4]{1,0:T(8,128)(4,1)S(1)} %copy.10), kind=kLoop, calls=%fused_computation.3 | loop fusion | flops 1638400 | bytes 6553632 | tf_op jit(solution)/shard_map/jit(_take)/select_n | solution.py:18
  17.6 80.5 %all_to_all.15 = bf16[8,4,80,640]{3,2,1,0:T(8,128)(2,1)S(1)} all-to-all(bf16[8,4,80,640]{3,2,1,0:T(8,128)(2,1)S(1)} %broadcast_select_fusion), channel_id=1, replica_groups=mesh['row'=4,'col'=8] {'col'}, dimensions={0} | all-to-all | bytes 6553600 | tf_op jit(solution)/shard_map/all_to_all | solution.py:21
  98.1 0.3 copy.12
  98.4 4.4 %convolution_convert_fusion = bf16[2560,640]{1,0:T(8,128)(2,1)} fusion(bf16[2560,640]{1,0:T(8,128)(2,1)S(1)} %bitcast.35, bf16[1,640,640]{2,1,0:T(8,128)(2,1)S(1)} %copy-done), kind=kOutput, calls=%fused_computation.2 | convolution fusion | flops 2098790400 | bytes 7372800 | tf_op jit(solution)/shard_map/dot_general | solution.py:22
  102.8 0.0 reduce-scatter.3.cloned.1.call-update
  102.9 0.0 reduce-scatter.5.cloned.1.call-start
  102.9 44.1 %reduce-scatter.3.cloned.1.call-done = bf16[640,640]{1,0:T(8,128)(2,1)} async-done(((bf16[2560,640]{1,0:T(8,128)(2,1)}), bf16[640,640]{1,0:T(8,128)(2,1)}) %reduce-scatter.3.cloned.1.call-update) | async-done | bytes 819216 | tf_op jit(solution)/shard_map/reduce_scatter | solution.py:25
  147.0 3.0 %fusion = bf16[640,640]{0,1:T(8,128)(2,1)} fusion(bf16[1,640,640]{2,1,0:T(8,128)(2,1)S(1)} %copy-done, bf16[640,640]{1,0:T(8,128)(2,1)} %reduce-scatter.3.cloned.1.call-done), kind=kOutput, calls=%fused_computation.7 | convolution fusion | flops 525926400 | bytes 2457600 | tf_op jit(solution)/shard_map/dot_general | solution.py:32
  150.0 0.0 reduce-scatter.5.cloned.1.call-update
  150.1 1.0 fusion.3
  151.1 25.4 %reduce-scatter.5.cloned.1.call-done = bf16[640,160]{0,1:T(8,128)(2,1)} async-done(((bf16[640,640]{0,1:T(8,128)(2,1)}), bf16[640,160]{0,1:T(8,128)(2,1)}) %reduce-scatter.5.cloned.1.call-update) | async-done | bytes 204816 | tf_op jit(solution)/shard_map/reduce_scatter | solution.py:35
  176.5 1.7 fusion.4
  (8 shorter events, 0.0 us)
Async XLA Ops:
  7.2 91.2 %copy-start = (bf16[1,640,640]{2,1,0:T(8,128)(2,1)S(1)}, bf16[1,640,640]{2,1,0:T(8,128)(2,1)}, u32[]{:S(2)}) copy-start(bf16[1,640,640]{2,1,0:T(8,128)(2,1)} %param.8) | copy-start | bytes 2457604
  7.2 139.8 %reduce-scatter.3.cloned.1.call-start = ((), (), s32[]{:S(2)}) async-start(), calls=%async_computation.3 | async-start | bytes 4096000 | tf_op jit(solution)/shard_map/reduce_scatter | solution.py:25
  102.9 73.7 %copy-start.2 = (f32[1,640,160]{1,2,0:T(8,128)S(1)}, f32[1,640,160]{1,2,0:T(8,128)}, u32[]{:S(2)}) copy-start(f32[1,640,160]{1,2,0:T(8,128)} %param.9) | copy-start | bytes 1228804
  102.9 73.7 %reduce-scatter.5.cloned.1.call-start = ((), (), s32[]{:S(2)}) async-start(), calls=%async_computation.4 | async-start | bytes 1024000 | tf_op jit(solution)/shard_map/reduce_scatter | solution.py:35
  147.0 3.1 %copy-start.1 = (bf16[640,640]{1,0:T(8,128)(2,1)S(1)}, bf16[640,640]{1,0:T(8,128)(2,1)}, u32[]{:S(2)}) copy-start(bf16[640,640]{1,0:T(8,128)(2,1)} %reduce-scatter.3.cloned.1.call-done) | copy-start | bytes 2457604
Sparse Core Ops, SparseCore 0:
  103.0 43.9 reduce-scatter.2
  150.2 26.2 reduce-scatter.4
where the time goes:
time: 185 us
  blocking collectives  80.5 us (44%)
  waiting for transfers between devices  69.5 us (38%)
  between operations  14.1 us (8%)
  matrix products  7.48 us (4%)
  other arithmetic  7.38 us (4%)
  local copies, waits for them, and re-layouts  6.03 us (3%)
    all_to_all x1, blocking collectives, body(): lax.all_to_all(outgoing, 'col', split_axis=0, concat_axis=2, tiled=True)  80.5 us
    reduce_scatter x1, waiting for transfers between devices, body(): lax.psum_scatter(slot_terms.reshape(-1, block_width).astype(jnp.bfloat16)...  44.1 us
    reduce_scatter x1, waiting for transfers between devices, body(): lax.psum_scatter(partial_terms.astype(jnp.bfloat16), 'row', scatter_dimen...  25.4 us
    dot_general x1, matrix products, body(): lax.dot_general(received[0], factor_block, (((2,), (0,)), ((), ())), pref...  4.45 us
  transfers between devices with their start and end apart: 2, of which 2 were waited for; matrix products, arithmetic and copies ran while one was open for 1% of the time, Pallas kernels for 0%

commit v1 on v0

v1 whole, which is shorter than its diff:
```python
import functools

import jax
import jax.numpy as jnp
from jax import lax
from jax.experimental import pallas as pl
from jax.experimental.pallas import tpu as pltpu
from jax.sharding import PartitionSpec as P

MESH = pl.DeviceIdType.MESH


def gather_kernel(owner_ref, struct_ref, sig_ref, out_ref):
    r = lax.axis_index("row")
    rows = sig_ref.shape[1]
    width = out_ref.shape[2]
    groups = sig_ref.shape[2] // width

    @pl.loop(0, struct_ref.shape[0])
    def _(k):
        column = owner_ref[struct_ref[k, r]] - r * groups
        lanes = pl.ds(pl.multiple_of(column * width, 128), width)
        for a in range(struct_ref.shape[1]):
            out_ref[k, a * rows : (a + 1) * rows, :] = sig_ref[struct_ref[k, a], :, lanes]


def kernel(
    nr, nc, outgoing, full_ref, fac_ref, diag_ref, off_ref, out_ref,
    recv, terms, rs_recv, total, pieces, p_recv,
    a_send, a_recv, b_send, b_recv, d_send, d_recv,
):
    r = lax.axis_index("row")
    c = lax.axis_index("col")
    rows = fac_ref.shape[1]
    width = full_ref.shape[1]
    strip = width // nr

    def flipped(s):
        result = 0
        bit = 1
        while bit < nc:
            mine = (c // bit) % 2
            other = (s // bit) % 2
            result = result + bit * (mine + other - 2 * mine * other)
            bit *= 2
        return result

    barrier = pltpu.get_barrier_semaphore()
    for d in range(1, nc):
        pl.semaphore_signal(barrier, inc=1, device_id=(r, lax.rem(c + d, nc)), device_id_type=MESH)
    for d in range(1, nr):
        pl.semaphore_signal(barrier, inc=1, device_id=(lax.rem(r + d, nr), c), device_id_type=MESH)

    def sigma_copy(s):
        k = flipped(s)
        return pltpu.make_async_remote_copy(
            src_ref=outgoing.at[k], dst_ref=recv.at[c], send_sem=a_send.at[k], recv_sem=a_recv.at[c],
            device_id=(r, k), device_id_type=MESH,
        )

    def sigma_wait(k):
        pltpu.make_async_remote_copy(
            src_ref=outgoing.at[k], dst_ref=recv.at[k], send_sem=a_send.at[k], recv_sem=a_recv.at[k],
            device_id=(r, k), device_id_type=MESH,
        ).wait_recv()

    def term_copy(i, d):
        to = lax.rem(r + d, nr)
        return pltpu.make_async_remote_copy(
            src_ref=terms.at[i, pl.ds(to * rows, rows)], dst_ref=rs_recv.at[d - 1, i],
            send_sem=b_send.at[d - 1, i], recv_sem=b_recv.at[d - 1, i],
            device_id=(to, c), device_id_type=MESH,
        )

    def piece_copy(d):
        to = lax.rem(r + d, nr)
        return pltpu.make_async_remote_copy(
            src_ref=pieces.at[d - 1], dst_ref=p_recv.at[d - 1],
            send_sem=d_send.at[d - 1], recv_sem=d_recv.at[d - 1],
            device_id=(to, c), device_id_type=MESH,
        )

    pl.semaphore_wait(barrier, nc - 1 + nr - 1)

    @pl.loop(0, nc - 1)
    def _(t):
        sigma_copy(nc - 1 - t).start()

    total[...] = jnp.zeros_like(total)

    def finish(s):
        i = flipped(s)
        for d in range(1, nr):
            term_copy(i, d).wait_recv()
        acc = terms[i, pl.ds(r * rows, rows)].astype(jnp.float32)
        for d in range(1, nr):
            acc = acc + rs_recv[d - 1, i].astype(jnp.float32)
        block = (-acc).astype(jnp.bfloat16)
        off_ref[i] = block
        total[...] += lax.dot_general(
            block, fac_ref[i], (((0,), (0,)), ((), ())), preferred_element_type=jnp.float32
        )

    @pl.loop(0, nc)
    def _(s):
        i = flipped(s)

        @pl.when(s > 0)
        def _():
            sigma_wait(i)

        def multiply(block):
            product = jnp.dot(block, full_ref[...], preferred_element_type=jnp.float32)
            terms[i] = product.astype(jnp.bfloat16)

        @pl.when(s == 0)
        def _():
            multiply(outgoing[c])

        @pl.when(s > 0)
        def _():
            multiply(recv[i])

        for d in range(1, nr):
            term_copy(i, d).start()

        @pl.when(s > 0)
        def _():
            finish(s - 1)

    finish(nc - 1)
    for d in range(1, nr):
        to = lax.rem(r + d, nr)
        pieces[d - 1] = total[pl.ds(pl.multiple_of(to * strip, 8), strip), :].astype(jnp.bfloat16)
        piece_copy(d).start()
    acc = total[pl.ds(pl.multiple_of(r * strip, 8), strip), :]
    for d in range(1, nr):
        piece_copy(d).wait_recv()
        acc = acc + p_recv[d - 1].astype(jnp.float32)
    out_ref[...] = diag_ref[...] - acc

    @pl.loop(1, nc)
    def _(s):
        sigma_copy(s).wait_send()

    @pl.loop(0, nc)
    def _(i):
        for d in range(1, nr):
            term_copy(i, d).wait_send()

    for d in range(1, nr):
        piece_copy(d).wait_send()


def body(nr, nc, sigma_anc, owner, structure, factor, diag_inv):
    rows = sigma_anc.shape[1]
    width = factor.shape[2]
    strip = width // nr
    full = factor[0]
    cut = full.reshape(nc, rows, width)
    padded = -(-rows // 16) * 16
    if padded != rows:
        extra = (0, 0), (0, padded - rows), (0, 0)
        sigma_anc, cut = jnp.pad(sigma_anc, extra), jnp.pad(cut, extra)
    vmem = pl.BlockSpec(memory_space=pltpu.VMEM)
    smem = pl.BlockSpec(memory_space=pltpu.SMEM)
    dma = pltpu.SemaphoreType.DMA
    outgoing = pl.pallas_call(
        gather_kernel,
        out_shape=jax.ShapeDtypeStruct((nc, nr * padded, width), jnp.bfloat16),
        in_specs=[smem, smem, vmem],
        out_specs=vmem,
        compiler_params=pltpu.CompilerParams(vmem_limit_bytes=32 * 1024 * 1024),
    )(owner, structure, sigma_anc)
    off, diag = pl.pallas_call(
        functools.partial(kernel, nr, nc),
        out_shape=(
            jax.ShapeDtypeStruct((nc, padded, width), jnp.bfloat16),
            jax.ShapeDtypeStruct((strip, width), jnp.float32),
        ),
        in_specs=[vmem, vmem, vmem, vmem],
        out_specs=(vmem, vmem),
        scratch_shapes=[
            pltpu.VMEM((nc, nr * padded, width), jnp.bfloat16),
            pltpu.VMEM((nc, nr * padded, width), jnp.bfloat16),
            pltpu.VMEM((nr - 1, nc, padded, width), jnp.bfloat16),
            pltpu.VMEM((width, width), jnp.float32),
            pltpu.VMEM((nr - 1, strip, width), jnp.bfloat16),
            pltpu.VMEM((nr - 1, strip, width), jnp.bfloat16),
            dma((nc,)), dma((nc,)), dma((nr - 1, nc)), dma((nr - 1, nc)), dma((nr - 1,)), dma((nr - 1,)),
        ],
        compiler_params=pltpu.CompilerParams(
            collective_id=0, has_side_effects=True, vmem_limit_bytes=60 * 1024 * 1024
        ),
    )(outgoing, full, cut, diag_inv[0].T)
    return off[:, :rows].reshape(1, width, width), diag.T[None]


def solution(mesh):
    return jax.shard_map(
        functools.partial(body, mesh.shape["row"], mesh.shape["col"]),
        mesh=mesh,
        in_specs=(P(None, "col", "row"), P(), P(), P("col", "row", None), P("col", None, "row")),
        out_specs=(P("col", "row", None), P("col", None, "row")),
        check_vma=False,
    )
```

time: 185 us -> 123 us (0.66)
  Pallas kernels: 0 us -> 113 us
  blocking collectives: 80.5 us -> 0 us
  waiting for transfers between devices: 69.5 us -> 0 us
  between operations: 14.1 us -> 0.66 us
  matrix products: 7.48 us -> 0 us
  other arithmetic: 7.38 us -> 0 us
  local copies, waits for them, and re-layouts: 6.03 us -> 8.38 us
    pallas_call x0 -> x2, Pallas kernels: none -> 113 us  [the longest x1 112 us: body(): pl.pallas_call(functools.partial(kernel, nr, nc), out_shape=(jax.ShapeDty...]
    all_to_all x1 -> x0, blocking collectives: 80.5 us -> none  [body(): lax.all_to_all(outgoing, 'col', split_axis=0, concat_axis=2, tiled=True)]
    reduce_scatter x2 -> x0, waiting for transfers between devices: 69.5 us -> none  [the longest x1 44.1 us: body(): lax.psum_scatter(slot_terms.reshape(-1, block_width).astype(jnp.bfloat16)...]
    unnamed x6 -> x9, local copies, waits for them, and re-layouts: 0.02 us -> 8.38 us
    dot_general x2 -> x0, matrix products: 7.48 us -> none  [the longest x1 4.45 us: body(): lax.dot_general(received[0], factor_block, (((2,), (0,)), ((), ())), pref...]
    gather x2 -> x0, local copies, waits for them, and re-layouts: 3.91 us -> none  [the longest x1 2.62 us: body(): outgoing = jnp.take(flattened, indices.reshape(-1), axis=0)]
    select_n x3 -> x0, other arithmetic: 3.09 us -> none  [the longest x2 2.34 us: body(): outgoing = jnp.take(flattened, indices.reshape(-1), axis=0)]
    broadcast_in_dim x2 -> x0, other arithmetic: 2.75 us -> none  [body(): return (offdiag[None], diagblock[None])]
  transfers between devices with their start and end apart: 2 -> 0, of which waited for: 2 -> 0; matrix products, arithmetic and copies ran while one was open for 1% -> 0% of each run, Pallas kernels for 0% -> 0%
where the time goes in v1:
time: 123 us; the launch traced here: 122 us
  Pallas kernels  113 us (92%)
  local copies, waits for them, and re-layouts  8.38 us (7%)
    pallas_call x1, Pallas kernels, body(): pl.pallas_call(functools.partial(kernel, nr, nc), out_shape=(jax.ShapeDty...  112 us
    unnamed x9, local copies, waits for them, and re-layouts  8.38 us

profile of v1, /device:TPU:0, one launch (start us, length us, event | category | flops | bytes accessed | tf_op | source)
XLA Modules:
  0.0 122.3 jit_solution(15039372816198300587)
XLA Ops:
  0.6 0.8 copy.7.struct_ref
  1.4 0.0 copy-start.1
  1.4 1.4 %copy-done.1 = bf16[8,80,1280]{2,1,0:T(8,128)(2,1)S(1)} copy-done((bf16[8,80,1280]{2,1,0:T(8,128)(2,1)S(1)}, bf16[8,80,1280]{2,1,0:T(8,128)(2,1)}, u32[]{:S(2)}) %copy-start.1) | copy-done | bytes 1638424
  2.8 0.0 copy-start.2
  2.8 0.7 copy-done.2
  3.5 1.0 shard_map.68.outgoing
  4.4 0.0 copy-start
  4.5 1.7 %copy-done = bf16[8,320,640]{2,1,0:T(8,128)(2,1)} copy-done((bf16[8,320,640]{2,1,0:T(8,128)(2,1)}, bf16[8,320,640]{2,1,0:T(8,128)(2,1)S(1)}, u32[]{:S(2)}) %copy-start) | copy-done | bytes 3276824
  6.1 112.3 %shard_map.69 = (bf16[8,80,640]{2,1,0:T(8,128)(2,1)}, f32[160,640]{1,0:T(8,128)}) custom-call(bf16[8,320,640]{2,1,0:T(8,128)(2,1)} %copy-done, bf16[640,640]{1,0:T(8,128)(2,1)} %bitcast.9, bf16[8,80,640]{2,1,0:T(8,128)(2,1)} %bitcast.10, f32[160,640]{1,0:T(8,128)} %bitcast.13), custom_call_target="tpu_custom_call" | custom-call | tf_op jit(solution)/shard_map/pallas_call | solution.py:175
  118.4 2.1 %copy.10 = bf16[1,640,640]{2,1,0:T(8,128)(2,1)} copy(bf16[1,640,640]{2,1,0:T(8,128)(2,1)} %bitcast.11) | data formatting | bytes 1638400
  120.5 1.8 %copy.11 = f32[1,640,160]{1,2,0:T(8,128)} copy(f32[1,640,160]{1,2,0:T(8,128)} %bitcast.12) | data formatting | bytes 819200
Async XLA Ops:
  1.4 1.4 %copy-start.1 = (bf16[8,80,1280]{2,1,0:T(8,128)(2,1)S(1)}, bf16[8,80,1280]{2,1,0:T(8,128)(2,1)}, u32[]{:S(2)}) copy-start(bf16[8,80,1280]{2,1,0:T(8,128)(2,1)} %sig_ref.1) | copy-start | bytes 4915204
  2.8 0.7 copy-start.2
  4.4 1.7 %copy-start = (bf16[8,320,640]{2,1,0:T(8,128)(2,1)}, bf16[8,320,640]{2,1,0:T(8,128)(2,1)S(1)}, u32[]{:S(2)}) copy-start(bf16[8,320,640]{2,1,0:T(8,128)(2,1)S(1)} %shard_map.68.outgoing) | copy-start | bytes 9830404

commit v2 on v1

--- a/solution.py
+++ b/solution.py
@@ -16,15 +16,15 @@
     width = out_ref.shape[2]
     groups = sig_ref.shape[2] // width
 
-    @pl.loop(0, struct_ref.shape[0])
+    @pl.loop(0, struct_ref.shape[1])
     def _(k):
-        column = owner_ref[struct_ref[k, r]] - r * groups
+        column = owner_ref[struct_ref[r, k]] - r * groups
         lanes = pl.ds(pl.multiple_of(column * width, 128), width)
-        for a in range(struct_ref.shape[1]):
-            out_ref[k, a * rows : (a + 1) * rows, :] = sig_ref[struct_ref[k, a], :, lanes]
-
-
-def kernel(
+        for a in range(struct_ref.shape[0]):
+            out_ref[k, a * rows : (a + 1) * rows, :] = sig_ref[struct_ref[a, k], :, lanes]
+
+
+def direct_kernel(
     nr, nc, outgoing, full_ref, fac_ref, diag_ref, off_ref, out_ref,
     recv, terms, rs_recv, total, pieces, p_recv,
     a_send, a_recv, b_send, b_recv, d_send, d_recv,
@@ -147,6 +147,273 @@
     def _(i):
         for d in range(1, nr):
             term_copy(i, d).wait_send()
+
+    for d in range(1, nr):
+        piece_copy(d).wait_send()
+
+
+CHUNKS = 4
+
+
+def line_kernel(
+    nr, nc, outgoing, full_ref, fac_ref, diag_ref, off_ref, out_ref,
+    panels, sent_rows, terms, rs_recv, stage, total, pieces, p_recv,
+    z_send, s_send, g_recv, a_send, a_recv, b_send, b_recv, o_send, o_recv, d_send, d_recv,
+):
+    r = lax.axis_index("row")
+    c = lax.axis_index("col")
+    rows = fac_ref.shape[1]
+    width = full_ref.shape[1]
+    strip = width // nr
+    depth = width // CHUNKS
+    z, q = c // 2, c % 2
+    half = z // 2
+    mid, end = 2 * (1 + half), 6 * half
+    mid_far, end_far = 2 * (2 - half), 6 * (1 - half)
+    here = 2 * z
+    sibling = here + 1 - q
+    is_end = 1 - (z + 1) // 2 % 2
+
+    barrier = pltpu.get_barrier_semaphore()
+    for d in range(1, nc):
+        pl.semaphore_signal(barrier, inc=1, device_id=(r, lax.rem(c + d, nc)), device_id_type=MESH)
+    for d in range(1, nr):
+        pl.semaphore_signal(barrier, inc=1, device_id=(lax.rem(r + d, nr), c), device_id_type=MESH)
+
+    def panel_copy(k, ch, to, sem):
+        part = panels.at[k, pl.ds(ch * depth, depth)]
+        return pltpu.make_async_remote_copy(
+            src_ref=part, dst_ref=part, send_sem=sem.at[k, ch], recv_sem=g_recv.at[k, ch],
+            device_id=(r, to), device_id_type=MESH,
+        )
+
+    def to_sibling(k, ch):
+        return panel_copy(k, ch, sibling, s_send)
+
+    def take(k, ch, onward=None):
+        panel_copy(k, ch, sibling, s_send).wait_recv()
+        if onward is not None:
+            panel_copy(k, ch, onward, z_send).start()
+        to_sibling(k, ch).start()
+
+    def from_sibling(k):
+        @pl.loop(0, CHUNKS)
+        def _(ch):
+            to_sibling(k, ch).wait_recv()
+
+    def rows_copy(t):
+        return pltpu.make_async_remote_copy(
+            src_ref=outgoing.at[mid + t], dst_ref=sent_rows.at[q], send_sem=a_send.at[t], recv_sem=a_recv.at[q],
+            device_id=(r, mid + t), device_id_type=MESH,
+        )
+
+    def rows_wait(t):
+        pltpu.make_async_remote_copy(
+            src_ref=outgoing.at[mid + t], dst_ref=sent_rows.at[t], send_sem=a_send.at[t], recv_sem=a_recv.at[t],
+            device_id=(r, end + t), device_id_type=MESH,
+        ).wait_recv()
+
+    def term_copy(job, d):
+        to = lax.rem(r + d, nr)
+        return pltpu.make_async_remote_copy(
+            src_ref=terms.at[job, pl.ds(to * rows, rows)], dst_ref=rs_recv.at[d - 1, job],
+            send_sem=b_send.at[d - 1, job], recv_sem=b_recv.at[d - 1, job],
+            device_id=(to, c), device_id_type=MESH,
+        )
+
+    def tile_copy(job, k):
+        return pltpu.make_async_remote_copy(
+            src_ref=stage.at[job], dst_ref=off_ref.at[c], send_sem=o_send.at[job], recv_sem=o_recv.at[c],
+            device_id=(r, k), device_id_type=MESH,
+        )
+
+    def tile_wait(i):
+        pltpu.make_async_remote_copy(
+            src_ref=stage.at[0], dst_ref=off_ref.at[i], send_sem=o_send.at[0], recv_sem=o_recv.at[i],
+            device_id=(r, i), device_id_type=MESH,
+        ).wait_recv()
+
+    def piece_copy(d):
+        to = lax.rem(r + d, nr)
+        return pltpu.make_async_remote_copy(
+            src_ref=pieces.at[d - 1], dst_ref=p_recv.at[d - 1],
+            send_sem=d_send.at[d - 1], recv_sem=d_recv.at[d - 1],
+            device_id=(to, c), device_id_type=MESH,
+        )
+
+    def multiply(job, left, right):
+        product = jnp.dot(left[...], right[...], preferred_element_type=jnp.float32)
+        terms[job] = product.astype(jnp.bfloat16)
+        for d in range(1, nr):
+            term_copy(job, d).start()
+
+    def issue(group, base):
+        @pl.loop(0, 2)
+        def _(t):
+            k = base + (q + t) % 2
+
+            @pl.when(t == 1)
+            def _():
+                from_sibling(k)
+
+            multiply(2 * group + t, outgoing.at[k], panels.at[k])
+
+    def summed(job):
+        for d in range(1, nr):
+            term_copy(job, d).wait_recv()
+        acc = terms[job, pl.ds(pl.multiple_of(r * rows, 16), rows)].astype(jnp.float32)
+        for d in range(1, nr):
+            acc = acc + rs_recv[d - 1, job].astype(jnp.float32)
+        return (-acc).astype(jnp.bfloat16)
+
+    def deliver(group, base):
+        @pl.loop(0, 2)
+        def _(t):
+            job = 2 * group + t
+            stage[job] = summed(job)
+            tile_copy(job, base + (q + t) % 2).start()
+
+    def deliver_own():
+        off_ref[c] = summed(0)
+        stage[1] = summed(1)
+        tile_copy(1, sibling).start()
+
+    panels[c] = full_ref[...]
+    pl.semaphore_wait(barrier, nc - 1 + nr - 1)
+
+    @pl.loop(0, CHUNKS)
+    def _(ch):
+        panel_copy(c, ch, (1 - is_end) * mid_far + is_end * mid + q, z_send).start()
+        to_sibling(c, ch).start()
+
+    issue(0, here)
+
+    @pl.when(is_end == 1)
+    def _():
+        @pl.loop(0, CHUNKS)
+        def _(ch):
+            panel_copy(c, ch, mid + q, z_send).wait_send()
+
+        @pl.loop(0, 2)
+        def _(t):
+            rows_copy(t).start()
+
+        @pl.loop(0, CHUNKS)
+        def _(ch):
+            take(mid_far + q, ch)
+
+    @pl.when(is_end == 0)
+    def _():
+        @pl.loop(0, CHUNKS)
+        def _(ch):
+            take(end + q, ch, mid_far + q)
+            take(mid_far + q, ch, end + q)
+
+        issue(1, end)
+
+    issue(2, mid_far)
+    deliver_own()
+
+    @pl.when(is_end == 1)
+    def _():
+        deliver(2, mid_far)
+
+        @pl.loop(0, CHUNKS)
+        def _(ch):
+            take(end_far + q, ch)
+
+    @pl.when(is_end == 0)
+    def _():
+        take(end_far + q, 0, end + q)
+        take(end_far + q, 1, end + q)
+        deliver(1, end)
+        take(end_far + q, 2, end + q)
+        deliver(2, mid_far)
+        take(end_far + q, 3, end + q)
+
+    issue(4, end_far)
+
+    @pl.when(is_end == 0)
+    def _():
+        @pl.loop(0, 2)
+        def _(t):
+            rows_wait(t)
+            multiply(6 + t, sent_rows.at[t], panels.at[c])
+
+    deliver(4, end_far)
+
+    @pl.when(is_end == 0)
+    def _():
+        @pl.loop(0, 2)
+        def _(t):
+            off_ref[end + t] = summed(6 + t)
+
+    def partial(start):
+        part = pl.ds(start, nc // 2)
+        return lax.dot_general(
+            off_ref[part].reshape(width // 2, width), fac_ref[part].reshape(width // 2, width),
+            (((0,), (0,)), ((), ())), preferred_element_type=jnp.float32,
+        )
+
+    tile_wait(sibling)
+
+    @pl.when(is_end == 1)
+    def _():
+        tile_wait(mid)
+        tile_wait(mid + 1)
+
+    total[...] = partial(half * (nc // 2))
+    for i in (mid_far, mid_far + 1, end_far, end_far + 1):
+        tile_wait(i)
+    total[...] += partial((1 - half) * (nc // 2))
+
+    for d in range(1, nr):
+        to = lax.rem(r + d, nr)
+        pieces[d - 1] = total[pl.ds(pl.multiple_of(to * strip, 8), strip), :].astype(jnp.bfloat16)
+        piece_copy(d).start()
+    acc = total[pl.ds(pl.multiple_of(r * strip, 8), strip), :]
+    for d in range(1, nr):
+        piece_copy(d).wait_recv()
+        acc = acc + p_recv[d - 1].astype(jnp.float32)
+    out_ref[...] = diag_ref[...] - acc
+
+    def sent(base):
+        @pl.loop(0, CHUNKS)
+        def _(ch):
+            panel_copy(base, ch, sibling, z_send).wait_send()
+
+    def shared(base):
+        @pl.loop(0, CHUNKS)
+        def _(ch):
+            to_sibling(base, ch).wait_send()
+
+    def done(job):
+        for d in range(1, nr):
+            term_copy(job, d).wait_send()
+
+    for k in (c, mid_far + q, end_far + q):
+        shared(k)
+    tile_copy(1, sibling).wait_send()
+    for group in (2, 4):
+        for t in range(2):
+            tile_copy(2 * group + t, sibling).wait_send()
+    for job in (0, 1, 4, 5, 8, 9):
+        done(job)
+
+    @pl.when(is_end == 1)
+    def _():
+        for t in range(2):
+            rows_copy(t).wait_send()
+
+    @pl.when(is_end == 0)
+    def _():
+        for k in (c, end + q, mid_far + q, end_far + q):
+            sent(k)
+        shared(end + q)
+        for t in range(2):
+            tile_copy(2 + t, sibling).wait_send()
+        for job in (2, 3, 6, 7):
+            done(job)
 
     for d in range(1, nr):
         piece_copy(d).wait_send()
@@ -171,26 +438,46 @@
         in_specs=[smem, smem, vmem],
         out_specs=vmem,
         compiler_params=pltpu.CompilerParams(vmem_limit_bytes=32 * 1024 * 1024),
-    )(owner, structure, sigma_anc)
-    off, diag = pl.pallas_call(
-        functools.partial(kernel, nr, nc),
-        out_shape=(
-            jax.ShapeDtypeStruct((nc, padded, width), jnp.bfloat16),
-            jax.ShapeDtypeStruct((strip, width), jnp.float32),
-        ),
-        in_specs=[vmem, vmem, vmem, vmem],
-        out_specs=(vmem, vmem),
-        scratch_shapes=[
+    )(owner, structure.T, sigma_anc)
+    results = (
+        jax.ShapeDtypeStruct((nc, padded, width), jnp.bfloat16),
+        jax.ShapeDtypeStruct((strip, width), jnp.float32),
+    )
+    line = nc == 8 and padded == rows and width % (16 * CHUNKS) == 0
+    ending = [
+        pltpu.VMEM((width, width), jnp.float32),
+        pltpu.VMEM((nr - 1, strip, width), jnp.bfloat16),
+        pltpu.VMEM((nr - 1, strip, width), jnp.bfloat16),
+    ]
+    if line:
+        run = functools.partial(line_kernel, nr, nc)
+        scratch = [
+            pltpu.VMEM((nc, width, width), jnp.bfloat16),
+            pltpu.VMEM((2, nr * rows, width), jnp.bfloat16),
+            pltpu.VMEM((10, nr * rows, width), jnp.bfloat16),
+            pltpu.VMEM((nr - 1, 10, rows, width), jnp.bfloat16),
+            pltpu.VMEM((10, rows, width), jnp.bfloat16),
+            *ending,
+            dma((nc, CHUNKS)), dma((nc, CHUNKS)), dma((nc, CHUNKS)), dma((2,)), dma((2,)),
+            dma((nr - 1, 10)), dma((nr - 1, 10)), dma((10,)), dma((nc,)), dma((nr - 1,)), dma((nr - 1,)),
+        ]
+    else:
+        run = functools.partial(direct_kernel, nr, nc)
+        scratch = [
             pltpu.VMEM((nc, nr * padded, width), jnp.bfloat16),
             pltpu.VMEM((nc, nr * padded, width), jnp.bfloat16),
             pltpu.VMEM((nr - 1, nc, padded, width), jnp.bfloat16),
-            pltpu.VMEM((width, width), jnp.float32),
-            pltpu.VMEM((nr - 1, strip, width), jnp.bfloat16),
-            pltpu.VMEM((nr - 1, strip, width), jnp.bfloat16),
+            *ending,
             dma((nc,)), dma((nc,)), dma((nr - 1, nc)), dma((nr - 1, nc)), dma((nr - 1,)), dma((nr - 1,)),
-        ],
+        ]
+    off, diag = pl.pallas_call(
+        run,
+        out_shape=results,
+        in_specs=[vmem, vmem, vmem, vmem],
+        out_specs=(vmem, vmem),
+        scratch_shapes=scratch,
         compiler_params=pltpu.CompilerParams(
-            collective_id=0, has_side_effects=True, vmem_limit_bytes=60 * 1024 * 1024
+            collective_id=1 if line else 0, has_side_effects=True, vmem_limit_bytes=60 * 1024 * 1024
         ),
     )(outgoing, full, cut, diag_inv[0].T)
     return off[:, :rows].reshape(1, width, width), diag.T[None]

time: 123 us -> 93.8 us (0.76)
  Pallas kernels: 113 us -> 84.6 us
    pallas_call x1, Pallas kernels: 112 us -> 83.6 us  [body(): pl.pallas_call(run, out_shape=results, in_specs=[vmem, vmem, vmem, vmem],...]
    unnamed x9 -> x10, local copies, waits for them, and re-layouts: 8.38 us -> 8.3 us
where the time goes in v2:
time: 93.8 us; the launch traced here: 93.5 us
  Pallas kernels  84.6 us (90%)
  local copies, waits for them, and re-layouts  8.3 us (9%)
    pallas_call x1, Pallas kernels, body(): pl.pallas_call(run, out_shape=results, in_specs=[vmem, vmem, vmem, vmem],...  83.6 us
    unnamed x10, local copies, waits for them, and re-layouts  8.3 us

profile of v2, /device:TPU:0, one launch (start us, length us, event | category | flops | bytes accessed | tf_op | source)
XLA Modules:
  0.0 93.5 jit_solution(5988950862725707281)
XLA Ops:
  0.6 0.0 copy-start.1
  0.6 1.4 %copy-done.1 = bf16[8,80,1280]{2,1,0:T(8,128)(2,1)S(1)} copy-done((bf16[8,80,1280]{2,1,0:T(8,128)(2,1)S(1)}, bf16[8,80,1280]{2,1,0:T(8,128)(2,1)}, u32[]{:S(2)}) %copy-start.1) | copy-done | bytes 1638424
  2.1 0.0 copy-start.2
  2.1 0.7 copy-done.2
  2.7 0.0 copy-start.3
  2.7 0.7 copy-done.3
  3.4 0.9 shard_map.68.outgoing
  4.3 0.0 copy-start
  4.4 1.7 %copy-done = bf16[8,320,640]{2,1,0:T(8,128)(2,1)} copy-done((bf16[8,320,640]{2,1,0:T(8,128)(2,1)}, bf16[8,320,640]{2,1,0:T(8,128)(2,1)S(1)}, u32[]{:S(2)}) %copy-start) | copy-done | bytes 3276824
  6.0 83.6 %shard_map.69 = (bf16[8,80,640]{2,1,0:T(8,128)(2,1)}, f32[160,640]{1,0:T(8,128)}) custom-call(bf16[8,320,640]{2,1,0:T(8,128)(2,1)} %copy-done, bf16[640,640]{1,0:T(8,128)(2,1)} %bitcast.11, bf16[8,80,640]{2,1,0:T(8,128)(2,1)} %bitcast.12, f32[160,640]{1,0:T(8,128)} %bitcast.15), custom_call_target="tpu_custom_call" | custom-call | tf_op jit(solution)/shard_map/pallas_call | solution.py:473
  89.7 2.1 %copy.9 = bf16[1,640,640]{2,1,0:T(8,128)(2,1)} copy(bf16[1,640,640]{2,1,0:T(8,128)(2,1)} %bitcast.13) | data formatting | bytes 1638400
  91.8 1.8 %copy.10 = f32[1,640,160]{1,2,0:T(8,128)} copy(f32[1,640,160]{1,2,0:T(8,128)} %bitcast.14) | data formatting | bytes 819200
Async XLA Ops:
  0.6 1.4 %copy-start.1 = (bf16[8,80,1280]{2,1,0:T(8,128)(2,1)S(1)}, bf16[8,80,1280]{2,1,0:T(8,128)(2,1)}, u32[]{:S(2)}) copy-start(bf16[8,80,1280]{2,1,0:T(8,128)(2,1)} %sig_ref.1) | copy-start | bytes 4915204
  2.1 0.7 copy-start.2
  2.7 0.7 copy-start.3
  4.3 1.7 %copy-start = (bf16[8,320,640]{2,1,0:T(8,128)(2,1)}, bf16[8,320,640]{2,1,0:T(8,128)(2,1)S(1)}, u32[]{:S(2)}) copy-start(bf16[8,320,640]{2,1,0:T(8,128)(2,1)S(1)} %shard_map.68.outgoing) | copy-start | bytes 9830404

commit v3 on v2

--- a/solution.py
+++ b/solution.py
@@ -156,13 +156,13 @@
 
 
 def line_kernel(
-    nr, nc, outgoing, full_ref, fac_ref, diag_ref, off_ref, out_ref,
-    panels, sent_rows, terms, rs_recv, stage, total, pieces, p_recv,
-    z_send, s_send, g_recv, a_send, a_recv, b_send, b_recv, o_send, o_recv, d_send, d_recv,
+    nr, nc, outgoing, full_ref, diag_ref, off_ref, out_ref,
+    panels, diag_here, sent_rows, terms, rs_recv, stage, total, pieces, p_recv,
+    z_send, s_send, g_recv, a_send, a_recv, b_send, b_recv, o_send, o_recv, d_send, d_recv, load,
 ):
     r = lax.axis_index("row")
     c = lax.axis_index("col")
-    rows = fac_ref.shape[1]
+    rows = outgoing.shape[1] // nr
     width = full_ref.shape[1]
     strip = width // nr
     depth = width // CHUNKS
@@ -174,6 +174,11 @@
     sibling = here + 1 - q
     is_end = 1 - (z + 1) // 2 % 2
 
+    load_panel = pltpu.make_async_copy(full_ref, panels.at[c], load.at[0])
+    load_panel.start()
+    load_diag = pltpu.make_async_copy(diag_ref, diag_here, load.at[1])
+    load_diag.start()
+
     barrier = pltpu.get_barrier_semaphore()
     for d in range(1, nc):
         pl.semaphore_signal(barrier, inc=1, device_id=(r, lax.rem(c + d, nc)), device_id_type=MESH)
@@ -278,8 +283,13 @@
         stage[1] = summed(1)
         tile_copy(1, sibling).start()
 
-    panels[c] = full_ref[...]
     pl.semaphore_wait(barrier, nc - 1 + nr - 1)
+
+    @pl.when(is_end == 1)
+    def _():
+        rows_copy(q).start()
+
+    load_panel.wait()
 
     @pl.loop(0, CHUNKS)
     def _(ch):
@@ -294,25 +304,27 @@
         def _(ch):
             panel_copy(c, ch, mid + q, z_send).wait_send()
 
-        @pl.loop(0, 2)
-        def _(t):
-            rows_copy(t).start()
+        rows_copy(1 - q).start()
 
         @pl.loop(0, CHUNKS)
         def _(ch):
             take(mid_far + q, ch)
 
+        deliver_own()
+
     @pl.when(is_end == 0)
     def _():
-        @pl.loop(0, CHUNKS)
-        def _(ch):
-            take(end + q, ch, mid_far + q)
-            take(mid_far + q, ch, end + q)
-
-        issue(1, end)
+        take(mid_far + q, 0, end + q)
+        rows_wait(q)
+        multiply(6, sent_rows.at[q], panels.at[c])
+        take(mid_far + q, 1, end + q)
+        take(end + q, 0, mid_far + q)
+        take(mid_far + q, 2, end + q)
+        deliver_own()
+        take(end + q, 1, mid_far + q)
+        take(mid_far + q, 3, end + q)
 
     issue(2, mid_far)
-    deliver_own()
 
     @pl.when(is_end == 1)
     def _():
@@ -324,34 +336,36 @@
 
     @pl.when(is_end == 0)
     def _():
+        take(end + q, 2, mid_far + q)
+        take(end + q, 3, mid_far + q)
+        issue(1, end)
         take(end_far + q, 0, end + q)
+        deliver(2, mid_far)
         take(end_far + q, 1, end + q)
+        take(end_far + q, 2, end + q)
         deliver(1, end)
-        take(end_far + q, 2, end + q)
-        deliver(2, mid_far)
         take(end_far + q, 3, end + q)
 
     issue(4, end_far)
+
+    @pl.when(is_end == 0)
+    def _():
+        rows_wait(1 - q)
+        multiply(7, sent_rows.at[1 - q], panels.at[c])
+
+    deliver(4, end_far)
 
     @pl.when(is_end == 0)
     def _():
         @pl.loop(0, 2)
         def _(t):
-            rows_wait(t)
-            multiply(6 + t, sent_rows.at[t], panels.at[c])
-
-    deliver(4, end_far)
-
-    @pl.when(is_end == 0)
-    def _():
-        @pl.loop(0, 2)
-        def _(t):
-            off_ref[end + t] = summed(6 + t)
+            off_ref[end + (q + t) % 2] = summed(6 + t)
 
     def partial(start):
         part = pl.ds(start, nc // 2)
         return lax.dot_general(
-            off_ref[part].reshape(width // 2, width), fac_ref[part].reshape(width // 2, width),
+            off_ref[part].reshape(width // 2, width),
+            panels[c, pl.ds(pl.multiple_of(start * rows, 16), width // 2)],
             (((0,), (0,)), ((), ())), preferred_element_type=jnp.float32,
         )
 
@@ -375,7 +389,8 @@
     for d in range(1, nr):
         piece_copy(d).wait_recv()
         acc = acc + p_recv[d - 1].astype(jnp.float32)
-    out_ref[...] = diag_ref[...] - acc
+    load_diag.wait()
+    out_ref[...] = diag_here[...] - acc
 
     def sent(base):
         @pl.loop(0, CHUNKS)
@@ -437,7 +452,7 @@
         out_shape=jax.ShapeDtypeStruct((nc, nr * padded, width), jnp.bfloat16),
         in_specs=[smem, smem, vmem],
         out_specs=vmem,
-        compiler_params=pltpu.CompilerParams(vmem_limit_bytes=32 * 1024 * 1024),
+        compiler_params=pltpu.CompilerParams(vmem_limit_bytes=24 * 1024 * 1024),
     )(owner, structure.T, sigma_anc)
     results = (
         jax.ShapeDtypeStruct((nc, padded, width), jnp.bfloat16),
@@ -449,19 +464,23 @@
         pltpu.VMEM((nr - 1, strip, width), jnp.bfloat16),
         pltpu.VMEM((nr - 1, strip, width), jnp.bfloat16),
     ]
+    anywhere = pl.BlockSpec(memory_space=pl.ANY)
     if line:
+        operands, places = (outgoing, full, diag_inv[0].T), [vmem, anywhere, anywhere]
         run = functools.partial(line_kernel, nr, nc)
         scratch = [
             pltpu.VMEM((nc, width, width), jnp.bfloat16),
+            pltpu.VMEM((strip, width), jnp.float32),
             pltpu.VMEM((2, nr * rows, width), jnp.bfloat16),
             pltpu.VMEM((10, nr * rows, width), jnp.bfloat16),
             pltpu.VMEM((nr - 1, 10, rows, width), jnp.bfloat16),
             pltpu.VMEM((10, rows, width), jnp.bfloat16),
             *ending,
             dma((nc, CHUNKS)), dma((nc, CHUNKS)), dma((nc, CHUNKS)), dma((2,)), dma((2,)),
-            dma((nr - 1, 10)), dma((nr - 1, 10)), dma((10,)), dma((nc,)), dma((nr - 1,)), dma((nr - 1,)),
+            dma((nr - 1, 10)), dma((nr - 1, 10)), dma((10,)), dma((nc,)), dma((nr - 1,)), dma((nr - 1,)), dma((2,)),
         ]
     else:
+        operands, places = (outgoing, full, cut, diag_inv[0].T), [vmem] * 4
         run = functools.partial(direct_kernel, nr, nc)
         scratch = [
             pltpu.VMEM((nc, nr * padded, width), jnp.bfloat16),
@@ -473,13 +492,13 @@
     off, diag = pl.pallas_call(
         run,
         out_shape=results,
-        in_specs=[vmem, vmem, vmem, vmem],
+        in_specs=places,
         out_specs=(vmem, vmem),
         scratch_shapes=scratch,
         compiler_params=pltpu.CompilerParams(
-            collective_id=1 if line else 0, has_side_effects=True, vmem_limit_bytes=60 * 1024 * 1024
+            collective_id=1 if line else 0, has_side_effects=True, vmem_limit_bytes=(32 if line else 60) * 1024 * 1024
         ),
-    )(outgoing, full, cut, diag_inv[0].T)
+    )(*operands)
     return off[:, :rows].reshape(1, width, width), diag.T[None]
 
 

time: 93.8 us -> 100 us (1.066)
  Pallas kernels: 84.6 us -> 94.6 us
  local copies, waits for them, and re-layouts: 8.3 us -> 4.71 us
    pallas_call x1, Pallas kernels: 83.6 us -> 93.6 us  [body(): pl.pallas_call(run, out_shape=results, in_specs=places, out_specs=(vmem,...]
    unnamed x10 -> x12, local copies, waits for them, and re-layouts: 8.3 us -> 4.71 us
where the time goes in v3:
time: 100 us; the launch traced here: 99.9 us
  Pallas kernels  94.6 us (95%)
  local copies, waits for them, and re-layouts  4.71 us (5%)
    pallas_call x1, Pallas kernels, body(): pl.pallas_call(run, out_shape=results, in_specs=places, out_specs=(vmem,...  93.6 us
    unnamed x12, local copies, waits for them, and re-layouts  4.71 us

profile of v3, /device:TPU:0, one launch (start us, length us, event | category | flops | bytes accessed | tf_op | source)
XLA Modules:
  0.0 99.9 jit_solution(15025345903929211840)
XLA Ops:
  0.6 0.0 copy-start
  0.6 1.4 %copy-done = bf16[8,80,1280]{2,1,0:T(8,128)(2,1)S(1)} copy-done((bf16[8,80,1280]{2,1,0:T(8,128)(2,1)S(1)}, bf16[8,80,1280]{2,1,0:T(8,128)(2,1)}, u32[]{:S(2)}) %copy-start) | copy-done | bytes 1638424
  2.1 0.0 copy-start.3
  2.1 0.7 copy-done.3
  2.7 0.0 copy-start.4
  2.7 0.7 copy-done.4
  3.4 0.0 copy-start.1
  3.4 0.0 copy-start.2
  3.4 0.9 shard_map.68.outgoing
  4.3 0.2 copy-done.1
  4.5 0.1 copy-done.2
  4.6 93.6 %shard_map.69 = (bf16[8,80,640]{2,1,0:T(8,128)(2,1)S(1)}, f32[160,640]{1,0:T(8,128)S(1)}) custom-call(bf16[8,320,640]{2,1,0:T(8,128)(2,1)S(1)} %shard_map.68.outgoing, bf16[640,640]{1,0:T(8,128)(2,1)S(1)} %bitcast.10, f32[160,640]{1,0:T(8,128)S(1)} %bitcast.11), custom_call_target="tpu_custom_call" | custom-call | tf_op jit(solution)/shard_map/pallas_call | solution.py:492
  98.3 0.9 copy.9
  99.2 0.8 copy.10
Async XLA Ops:
  0.6 1.4 %copy-start = (bf16[8,80,1280]{2,1,0:T(8,128)(2,1)S(1)}, bf16[8,80,1280]{2,1,0:T(8,128)(2,1)}, u32[]{:S(2)}) copy-start(bf16[8,80,1280]{2,1,0:T(8,128)(2,1)} %sig_ref.1) | copy-start | bytes 4915204
  2.1 0.7 copy-start.3
  2.7 0.7 copy-start.4
  3.4 1.1 %copy-start.1 = (bf16[1,640,640]{2,1,0:T(8,128)(2,1)S(1)}, bf16[1,640,640]{2,1,0:T(8,128)(2,1)}, u32[]{:S(2)}) copy-start(bf16[1,640,640]{2,1,0:T(8,128)(2,1)} %param.8) | copy-start | bytes 2457604
  3.4 1.2 %copy-start.2 = (f32[1,640,160]{1,2,0:T(8,128)S(1)}, f32[1,640,160]{1,2,0:T(8,128)}, u32[]{:S(2)}) copy-start(f32[1,640,160]{1,2,0:T(8,128)} %param.9) | copy-start | bytes 1228804

commit v4 on v2

--- a/solution.py
+++ b/solution.py
@@ -156,13 +156,13 @@
 
 
 def line_kernel(
-    nr, nc, outgoing, full_ref, fac_ref, diag_ref, off_ref, out_ref,
-    panels, sent_rows, terms, rs_recv, stage, total, pieces, p_recv,
-    z_send, s_send, g_recv, a_send, a_recv, b_send, b_recv, o_send, o_recv, d_send, d_recv,
+    nr, nc, outgoing, full_ref, diag_ref, off_ref, out_ref,
+    panels, diag_here, sent_rows, terms, rs_recv, stage, total, pieces, p_recv,
+    z_send, s_send, g_recv, a_send, a_recv, b_send, b_recv, o_send, o_recv, d_send, d_recv, load,
 ):
     r = lax.axis_index("row")
     c = lax.axis_index("col")
-    rows = fac_ref.shape[1]
+    rows = outgoing.shape[1] // nr
     width = full_ref.shape[1]
     strip = width // nr
     depth = width // CHUNKS
@@ -174,6 +174,11 @@
     sibling = here + 1 - q
     is_end = 1 - (z + 1) // 2 % 2
 
+    load_panel = pltpu.make_async_copy(full_ref, panels.at[c], load.at[0])
+    load_panel.start()
+    load_diag = pltpu.make_async_copy(diag_ref, diag_here, load.at[1])
+    load_diag.start()
+
     barrier = pltpu.get_barrier_semaphore()
     for d in range(1, nc):
         pl.semaphore_signal(barrier, inc=1, device_id=(r, lax.rem(c + d, nc)), device_id_type=MESH)
@@ -278,8 +283,9 @@
         stage[1] = summed(1)
         tile_copy(1, sibling).start()
 
-    panels[c] = full_ref[...]
     pl.semaphore_wait(barrier, nc - 1 + nr - 1)
+
+    load_panel.wait()
 
     @pl.loop(0, CHUNKS)
     def _(ch):
@@ -351,7 +357,8 @@
     def partial(start):
         part = pl.ds(start, nc // 2)
         return lax.dot_general(
-            off_ref[part].reshape(width // 2, width), fac_ref[part].reshape(width // 2, width),
+            off_ref[part].reshape(width // 2, width),
+            panels[c, pl.ds(pl.multiple_of(start * rows, 16), width // 2)],
             (((0,), (0,)), ((), ())), preferred_element_type=jnp.float32,
         )
 
@@ -375,7 +382,8 @@
     for d in range(1, nr):
         piece_copy(d).wait_recv()
         acc = acc + p_recv[d - 1].astype(jnp.float32)
-    out_ref[...] = diag_ref[...] - acc
+    load_diag.wait()
+    out_ref[...] = diag_here[...] - acc
 
     def sent(base):
         @pl.loop(0, CHUNKS)
@@ -437,7 +445,7 @@
         out_shape=jax.ShapeDtypeStruct((nc, nr * padded, width), jnp.bfloat16),
         in_specs=[smem, smem, vmem],
         out_specs=vmem,
-        compiler_params=pltpu.CompilerParams(vmem_limit_bytes=32 * 1024 * 1024),
+        compiler_params=pltpu.CompilerParams(vmem_limit_bytes=24 * 1024 * 1024),
     )(owner, structure.T, sigma_anc)
     results = (
         jax.ShapeDtypeStruct((nc, padded, width), jnp.bfloat16),
@@ -449,19 +457,23 @@
         pltpu.VMEM((nr - 1, strip, width), jnp.bfloat16),
         pltpu.VMEM((nr - 1, strip, width), jnp.bfloat16),
     ]
+    anywhere = pl.BlockSpec(memory_space=pl.ANY)
     if line:
+        operands, places = (outgoing, full, diag_inv[0].T), [vmem, anywhere, anywhere]
         run = functools.partial(line_kernel, nr, nc)
         scratch = [
             pltpu.VMEM((nc, width, width), jnp.bfloat16),
+            pltpu.VMEM((strip, width), jnp.float32),
             pltpu.VMEM((2, nr * rows, width), jnp.bfloat16),
             pltpu.VMEM((10, nr * rows, width), jnp.bfloat16),
             pltpu.VMEM((nr - 1, 10, rows, width), jnp.bfloat16),
             pltpu.VMEM((10, rows, width), jnp.bfloat16),
             *ending,
             dma((nc, CHUNKS)), dma((nc, CHUNKS)), dma((nc, CHUNKS)), dma((2,)), dma((2,)),
-            dma((nr - 1, 10)), dma((nr - 1, 10)), dma((10,)), dma((nc,)), dma((nr - 1,)), dma((nr - 1,)),
+            dma((nr - 1, 10)), dma((nr - 1, 10)), dma((10,)), dma((nc,)), dma((nr - 1,)), dma((nr - 1,)), dma((2,)),
         ]
     else:
+        operands, places = (outgoing, full, cut, diag_inv[0].T), [vmem] * 4
         run = functools.partial(direct_kernel, nr, nc)
         scratch = [
             pltpu.VMEM((nc, nr * padded, width), jnp.bfloat16),
@@ -473,13 +485,13 @@
     off, diag = pl.pallas_call(
         run,
         out_shape=results,
-        in_specs=[vmem, vmem, vmem, vmem],
+        in_specs=places,
         out_specs=(vmem, vmem),
         scratch_shapes=scratch,
         compiler_params=pltpu.CompilerParams(
-            collective_id=1 if line else 0, has_side_effects=True, vmem_limit_bytes=60 * 1024 * 1024
+            collective_id=1 if line else 0, has_side_effects=True, vmem_limit_bytes=(32 if line else 60) * 1024 * 1024
         ),
-    )(outgoing, full, cut, diag_inv[0].T)
+    )(*operands)
     return off[:, :rows].reshape(1, width, width), diag.T[None]
 
 

time: 93.8 us -> 87 us (0.928)
  local copies, waits for them, and re-layouts: 8.3 us -> 4.71 us
  Pallas kernels: 84.6 us -> 81.4 us
    unnamed x10 -> x12, local copies, waits for them, and re-layouts: 8.3 us -> 4.71 us
    pallas_call x1, Pallas kernels: 83.6 us -> 80.5 us  [body(): pl.pallas_call(run, out_shape=results, in_specs=places, out_specs=(vmem,...]
where the time goes in v4:
time: 87 us; the launch traced here: 86.8 us
  Pallas kernels  81.4 us (94%)
  local copies, waits for them, and re-layouts  4.71 us (5%)
    pallas_call x1, Pallas kernels, body(): pl.pallas_call(run, out_shape=results, in_specs=places, out_specs=(vmem,...  80.5 us
    unnamed x12, local copies, waits for them, and re-layouts  4.71 us

profile of v4, /device:TPU:0, one launch (start us, length us, event | category | flops | bytes accessed | tf_op | source)
XLA Modules:
  0.0 86.8 jit_solution(11331669038291194112)
XLA Ops:
  0.6 0.0 copy-start
  0.6 1.4 %copy-done = bf16[8,80,1280]{2,1,0:T(8,128)(2,1)S(1)} copy-done((bf16[8,80,1280]{2,1,0:T(8,128)(2,1)S(1)}, bf16[8,80,1280]{2,1,0:T(8,128)(2,1)}, u32[]{:S(2)}) %copy-start) | copy-done | bytes 1638424
  2.1 0.0 copy-start.3
  2.1 0.7 copy-done.3
  2.7 0.0 copy-start.4
  2.7 0.7 copy-done.4
  3.4 0.0 copy-start.1
  3.4 0.0 copy-start.2
  3.4 0.9 %shard_map.68.outgoing = bf16[8,320,640]{2,1,0:T(8,128)(2,1)S(1)} custom-call(s32[8]{0:T(128)S(1)} %copy-done.4, s32[4,8]{1,0:T(4,128)S(1)} %bitcast.13, bf16[8,80,1280]{2,1,0:T(8,128)(2,1)S(1)} %copy-done), custom_call_target="tpu_custom_call" | custom-call | tf_op jit(solution)/shard_map/pallas_call | solution.py:443
  4.3 0.2 copy-done.1
  4.5 0.1 copy-done.2
  4.6 80.5 %shard_map.69 = (bf16[8,80,640]{2,1,0:T(8,128)(2,1)S(1)}, f32[160,640]{1,0:T(8,128)S(1)}) custom-call(bf16[8,320,640]{2,1,0:T(8,128)(2,1)S(1)} %shard_map.68.outgoing, bf16[640,640]{1,0:T(8,128)(2,1)S(1)} %bitcast.10, f32[160,640]{1,0:T(8,128)S(1)} %bitcast.11), custom_call_target="tpu_custom_call" | custom-call | tf_op jit(solution)/shard_map/pallas_call | solution.py:485
  85.1 0.9 %copy.9 = bf16[1,640,640]{2,1,0:T(8,128)(2,1)} copy(bf16[1,640,640]{2,1,0:T(8,128)(2,1)S(1)} %bitcast.9) | data formatting | bytes 1638400
  86.0 0.8 copy.10
Async XLA Ops:
  0.6 1.4 %copy-start = (bf16[8,80,1280]{2,1,0:T(8,128)(2,1)S(1)}, bf16[8,80,1280]{2,1,0:T(8,128)(2,1)}, u32[]{:S(2)}) copy-start(bf16[8,80,1280]{2,1,0:T(8,128)(2,1)} %sig_ref.1) | copy-start | bytes 4915204
  2.1 0.7 copy-start.3
  2.7 0.7 copy-start.4
  3.4 1.1 %copy-start.1 = (bf16[1,640,640]{2,1,0:T(8,128)(2,1)S(1)}, bf16[1,640,640]{2,1,0:T(8,128)(2,1)}, u32[]{:S(2)}) copy-start(bf16[1,640,640]{2,1,0:T(8,128)(2,1)} %param.8) | copy-start | bytes 2457604
  3.4 1.2 %copy-start.2 = (f32[1,640,160]{1,2,0:T(8,128)S(1)}, f32[1,640,160]{1,2,0:T(8,128)}, u32[]{:S(2)}) copy-start(f32[1,640,160]{1,2,0:T(8,128)} %param.9) | copy-start | bytes 1228804
